TPU v7x, 32 devices: a whole 2x2x4 slice. The times are simulated.
32 devices in a mesh: cases: 2 (over y), wheel: 4 (over z), inst: 4 (over x, core).
Axes of the slice: x: 2, y: 2, z: 4, core: 2. Of those that a mesh axis runs over, the one named last changes fastest.
Arguments:
- state: float32 [16, 5, 1024, 128], P('inst', None, ('cases', 'wheel')), parts along dimension 2, as said below
- slot_blade: int32 [8], P(('cases', 'wheel')), parts along dimension 0, may hold values from 0 to 3, each once
- blade_class: int32 [8], P('cases'), parts along dimension 0, may hold values from 0 to 3
- face_index: int32 [8, 2, 128], P(('cases', 'wheel')), parts along dimension 0, may hold values from 0 to 127, as said below
- class_amplitude: float32 [4], replicated, may hold values from 0.3 to 1.2
- class_phase: float32 [4], replicated, may hold values from -3.140625 to 3.140625
Outputs:
- new_state: float32 [16, 5, 1024, 128], P('inst', None, ('cases', 'wheel')), parts along dimension 2
- last_residual: float32 [16, 5, 1024, 128], P('inst', None, ('cases', 'wheel')), parts along dimension 2
There are 2 independent parts, one for each index of `cases`. A program takes and returns all parts, laid end to end along the dimension named above; an argument that names none is the same for every part. Nothing has to cross between parts.
Inputs may be any that keep to these rules, and one draw needn't show every extreme that they name: `state`: density lies in [0.8, 1.2] and pressure is positive in every cell. `slot_blade`: each blade sits in exactly one slot. face_index[s, side, k] differs from k by at most one.
All inputs are finite; a program needn't handle non-finite values.
Results may differ from a plain program's by a relative error of at most 0.0003.
Values sent between devices are 32-bit elements; how exact they have to be, the bound alone decides.
A program may use at most 64 MiB of HBM per device.

v0:
```python
import math
import jax
import jax.numpy as jnp
from jax import lax
from jax.sharding import PartitionSpec as P

INST = 16
HEAT_RATIO = 1.4
TIME_STEP = 0.05
DISSIPATION = 2.0
FREQUENCY = 0.5


def padded_2(shard, sides, width):
    for axis, dim in sides:
        size, length = (lax.axis_size(axis), shard.shape[dim])
        up = [(i, (i + 1) % size) for i in range(size)]
        down = [(j, i) for i, j in up]
        last = lax.slice_in_dim(shard, length - width, length, axis=dim)
        initial = lax.slice_in_dim(shard, 0, width, axis=dim)
        before = lax.ppermute(last, axis, up)
        after = lax.ppermute(initial, axis, down)
        shard = jnp.concatenate([before, shard, after], axis=dim)
    return shard


def fluxes(field):
    density = field[:, 0]
    axial_mom = field[:, 1]
    pitch_mom = field[:, 2]
    radial_mom = field[:, 3]
    energy = field[:, 4]
    inverse = 1.0 / density
    axial_vel = axial_mom * inverse
    pitch_vel = pitch_mom * inverse
    pressure = (HEAT_RATIO - 1.0) * (
        energy
        - 0.5 * (axial_mom * axial_mom + pitch_mom * pitch_mom + radial_mom * radial_mom) * inverse
    )
    enthalpy = energy + pressure
    axial_flux = jnp.stack(
        [
            axial_mom,
            axial_mom * axial_vel + pressure,
            pitch_mom * axial_vel,
            radial_mom * axial_vel,
            enthalpy * axial_vel,
        ],
        1,
    )
    pitch_flux = jnp.stack(
        [
            pitch_mom,
            axial_mom * pitch_vel,
            pitch_mom * pitch_vel + pressure,
            radial_mom * pitch_vel,
            enthalpy * pitch_vel,
        ],
        1,
    )
    return (axial_flux, pitch_flux)


def spectral_matrix(count):
    steps_apart = jnp.arange(count)[:, None] - jnp.arange(count)[None, :]
    apart = steps_apart != 0
    angle = jnp.where(apart, math.pi / count * steps_apart.astype(jnp.float32), 1.0)
    parity = jnp.where(steps_apart % 2 == 0, 1.0, -1.0)
    return jnp.where(apart, 0.5 * parity * jnp.cos(angle) / jnp.sin(angle), 0.0)


def face_terms(left, right, flux_left, flux_right, speed):
    return (
        0.5 * (flux_left + flux_right)
        - speed * 0.5 * (left + right)
        - 0.5 * DISSIPATION * (right - left)
    )


def local_residual(field, extended, speed, spectral):
    axial_ext, pitch_ext = fluxes(extended)
    axial_flux = axial_ext[:, :, 1:-1, :]
    axial_pad = jnp.concatenate([axial_flux[..., :1], axial_flux, axial_flux[..., -1:]], axis=3)
    field_pad = jnp.concatenate([field[..., :1], field, field[..., -1:]], axis=3)
    axial_face = face_terms(
        field_pad[..., :-1], field_pad[..., 1:], axial_pad[..., :-1], axial_pad[..., 1:], 0.0
    )
    pitch_face = face_terms(
        extended[:, :, :-1],
        extended[:, :, 1:],
        pitch_ext[:, :, :-1],
        pitch_ext[:, :, 1:],
        speed[:, None, None, None],
    )
    return (
        -(axial_face[..., 1:] - axial_face[..., :-1])
        - (pitch_face[:, :, 1:] - pitch_face[:, :, :-1])
        - FREQUENCY * spectral
    )


def body(state, slot_blade, blade_class, face_index, class_amplitude, class_phase):
    per_dev = state.shape[0]
    own_start = lax.axis_index("inst") * per_dev
    blade = slot_blade[0]
    class_id = jnp.sum(jnp.where(jnp.arange(blade_class.shape[0]) == blade, blade_class, 0))
    class_pick = jnp.arange(class_amplitude.shape[0]) == class_id
    amplitude = jnp.sum(jnp.where(class_pick, class_amplitude, 0.0))
    phase = jnp.sum(jnp.where(class_pick, class_phase, 0.0))
    matrix = spectral_matrix(INST)
    face_row = face_index[0]
    instance = (own_start + jnp.arange(per_dev)).astype(jnp.float32)
    speed = amplitude * jnp.sin(2.0 * math.pi / INST * instance + phase)
    own_rows = lax.dynamic_slice_in_dim(matrix, own_start, per_dev, 0)

    def spectral_of(field):
        return jnp.einsum(
            "nm,mvjk->nvjk",
            own_rows,
            lax.all_gather(field, "inst", axis=0, tiled=True),
            precision=lax.Precision.HIGHEST,
        )

    def residual_of(field):
        padded = padded_2(field, (("wheel", 2),), 1)
        lower = jnp.take(padded[:, :, 0, :], face_row[0], axis=2)
        upper = jnp.take(padded[:, :, -1, :], face_row[1], axis=2)
        extended = jnp.concatenate([lower[:, :, None, :], field, upper[:, :, None, :]], axis=2)
        return local_residual(field, extended, speed, spectral_of(field))

    first = state + 0.5 * TIME_STEP * residual_of(state)
    last_residual = residual_of(first)
    new_state = state + TIME_STEP * last_residual
    return (new_state, last_residual)


def solution(mesh):
    placed = (
        P("inst", None, ("cases", "wheel"), None),
        P(("cases", "wheel")),
        P("cases"),
        P(("cases", "wheel"), None, None),
        P(),
        P(),
    )
    return jax.shard_map(
        body,
        mesh=mesh,
        in_specs=placed,
        out_specs=(
            P("inst", None, ("cases", "wheel"), None),
            P("inst", None, ("cases", "wheel"), None),
        ),
        check_vma=False,
    )
```

profile of v0, /device:TPU:0, one launch (start us, length us, event | category | flops | bytes accessed | tf_op | source)
XLA Modules:
  0.0 127.6 jit_solution(13102067222919137972)
XLA Ops:
  7.2 0.0 all-gather.3.cloned.1.call-start
  7.2 0.7 all-gather.3.cloned.1.call-update
  7.9 0.0 all-gather.5.cloned.1.call-start
  8.0 0.9 fusion.54
  8.9 0.0 copy-start.6
  8.9 0.0 copy-start.7
  8.9 0.0 copy-start.8
  8.9 3.1 %collective-permute-start = (f32[4,5,1,128]{3,2,1,0:T(1,128)S(1)}, f32[4,5,1,128]{3,2,1,0:T(1,128)S(1)}, u32[]{:S(2)}, u32[]{:S(2)}) collective-permute-start(f32[4,5,1,128]{3,2,1,0:T(1,128)S(1)} %get-tuple-element.43), channel_id=1, source_target_pairs={{0,4},{4,8},{8,12},{12,0},{1,5},{5,9},{9,13},{13,1},{2,6},{6,10},{... | collective-permute-start | bytes 30728 | tf_op jit(solution)/shard_map/ppermute | solution.py:21
  12.0 2.1 %collective-permute-start.1 = (f32[4,5,1,128]{3,2,1,0:T(1,128)S(1)}, f32[4,5,1,128]{3,2,1,0:T(1,128)S(1)}, u32[]{:S(2)}, u32[]{:S(2)}) collective-permute-start(f32[4,5,1,128]{3,2,1,0:T(1,128)S(1)} %get-tuple-element.44), channel_id=1, source_target_pairs={{4,0},{8,4},{12,8},{0,12},{5,1},{9,5},{13,9},{1,13},{6,2},{10,6},{... | collective-permute-start | bytes 30728 | tf_op jit(solution)/shard_map/ppermute | solution.py:22
  14.1 0.8 copy.63
  15.7 0.6 fusion.46
  16.3 1.3 %fusion.44 = f32[]{:T(128)} fusion(f32[4]{0:T(128)S(1)} %copy-done.7, s32[]{:T(128)} %fusion.46), kind=kLoop, calls=%fused_computation.106 | loop fusion | flops 11 | bytes 24 | tf_op jit(solution)/shard_map/reduce_sum | solution.py:108
  17.6 1.3 fusion.45
  18.9 2.2 %fusion.53 = (f32[4,5,128,1]{3,0,2,1:T(4,128)}, f32[4,5,128,1]{3,0,2,1:T(4,128)}) fusion(f32[4,5,128,128]{3,0,2,1:T(4,128)S(1)} %copy.63), kind=kLoop, calls=%fused_computation.114 | loop fusion | bytes 40960 | tf_op jit(solution)/shard_map/slice | solution.py:84
  21.2 1.3 %multiply_multiply_fusion = f32[4]{0:T(128)S(1)} fusion(f32[]{:T(128)} %fusion.45, s32[]{:T(128)S(6)} %mul.290, f32[]{:T(128)} %fusion.44), kind=kLoop, calls=%fused_computation.109 | loop fusion | flops 24 | bytes 28 | tf_op jit(solution)/shard_map/mul | solution.py:75
  22.5 0.2 copy.67
  22.7 0.8 gather_fusion
  23.5 0.1 copy.44
  23.6 0.2 copy.68
  23.8 0.8 gather_fusion.1
  24.5 0.1 copy.47
  24.7 0.3 pad_maximum_fusion.4
  25.0 0.3 add_dynamic-update-slice_fusion.3
  25.3 0.1 multiply_dynamic-update-slice_fusion.11
  25.4 0.2 multiply_dynamic-update-slice_fusion.8
  25.6 0.2 multiply_dynamic-update-slice_fusion.9
  25.9 0.1 slice.198
  26.0 0.1 multiply_dynamic-update-slice_fusion.7
  26.1 0.1 multiply_dynamic-update-slice_fusion.6
  26.2 0.7 fusion.50
  26.9 0.0 copy-start.1
  27.0 0.0 copy-start.2
  27.0 1.9 %fusion.30 = f32[4,5,129,128]{3,0,2,1:T(4,128)} fusion(f32[4,5,130,128]{3,0,2,1:T(4,128)S(1)} %multiply_dynamic-update-slice_fusion.6, f32[4,5,1,128]{3,0,2,1:T(4,128)S(1)} %select_bitcast_fusion.2, f32[4,5,128,128]{3,0,2,1:T(4,128)S(1)} %copy.63, f32[4,5,1,128]{3,0,2,1:T(4,128)S(1)} %select_bitcast_fusion.3, f32[4]{0:T(128)S(1)} %multiply_multiply_fusion), kind=kLoop, calls=%fused_computation.34 | loop fusion | flops 2972160 | bytes 5294096 | tf_op jit(solution)/shard_map/sub | solution.py:74
  28.9 0.1 copy-done.2
  28.9 4.3 %fusion.6 = f32[4,5,128,129]{3,0,2,1:T(4,128)} fusion(f32[4,5,128,128]{3,0,2,1:T(4,128)S(1)} %slice.198, f32[4,5,128,1]{3,0,2,1:T(4,128)S(1)} %get-tuple-element.33, f32[4,5,128,1]{3,0,2,1:T(4,128)S(1)} %get-tuple-element.32, f32[4,5,128,1]{3,0,2,1:T(4,128)S(1)} %copy-done.2, f32[4,5,128,128]{3,0,2,1:T(4,128)S(1)} %copy.63, f32[4,5,128,1]{3,0,2,1:T(4,128)S(1)} %copy-done.1), kind=kLoop, calls=%fused_computation.11 | loop fusion | flops 3632640 | bytes 3983360 | tf_op jit(solution)/shard_map/sub | solution.py:74
  33.3 19.5 %all-gather.3.cloned.1.call-done = f32[16,5,128,128]{3,2,1,0:T(8,128)} async-done(((f32[4,5,128,128]{3,2,1,0:T(8,128)}), f32[16,5,128,128]{3,2,1,0:T(8,128)}) %all-gather.3.cloned.1.call-update) | async-done | bytes 5242896 | tf_op jit(solution)/shard_map/all_gather | solution.py:120
  52.7 11.8 %fusion.35 = f32[4,5,128,128]{3,0,2,1:T(4,128)S(1)} fusion(f32[16,5,128,128]{3,2,1,0:T(8,128)} %all-gather.3.cloned.1.call-done, f32[4,5,129,128]{3,0,2,1:T(4,128)} %fusion.30, f32[4,5,128,129]{3,0,2,1:T(4,128)} %fusion.6, f32[16,16]{1,0:T(8,128)S(1)} %fusion.39, s32[]{:T(128)S(6)} %select_n.46, s32[16,16]{1,0:T(8,128)S(1)} %iota_subtract_fusion, ...), kind=kOutput, calls=%fused_computation.47 | convolution fusion | flops 65536576 | bytes 13113348 | tf_op jit(solution)/shard_map/nm,mvjk->nvjk/dot_general | solution.py:117
  64.6 1.2 copy.61
  65.8 0.0 all-gather.5.cloned.1.call-update
  65.8 1.5 %collective-permute-start.2 = (f32[4,5,1,128]{3,0,2,1:T(4,128)S(1)}, f32[4,5,1,128]{3,0,2,1:T(4,128)S(1)}, u32[]{:S(2)}, u32[]{:S(2)}) collective-permute-start(f32[4,5,1,128]{3,0,2,1:T(4,128)S(1)} %get-tuple-element.39), channel_id=1, source_target_pairs={{0,4},{4,8},{8,12},{12,0},{1,5},{5,9},{9,13},{13,1},{2,6},{6,10},{... | collective-permute-start | bytes 30728 | tf_op jit(solution)/shard_map/ppermute | solution.py:21
  67.3 2.3 %collective-permute-start.3 = (f32[4,5,1,128]{3,0,2,1:T(4,128)S(1)}, f32[4,5,1,128]{3,0,2,1:T(4,128)S(1)}, u32[]{:S(2)}, u32[]{:S(2)}) collective-permute-start(f32[4,5,1,128]{3,0,2,1:T(4,128)S(1)} %get-tuple-element.40), channel_id=1, source_target_pairs={{4,0},{8,4},{12,8},{0,12},{5,1},{9,5},{13,9},{1,13},{6,2},{10,6},{... | collective-permute-start | bytes 30728 | tf_op jit(solution)/shard_map/ppermute | solution.py:22
  69.7 2.3 %fusion.51 = (f32[4,5,128,1]{3,0,2,1:T(4,128)}, f32[4,5,128,1]{3,0,2,1:T(4,128)}) fusion(f32[4,5,128,128]{3,0,2,1:T(4,128)S(1)} %fusion.35), kind=kLoop, calls=%fused_computation.112 | loop fusion | bytes 40960 | tf_op jit(solution)/shard_map/slice | solution.py:84
  72.0 0.2 copy.57
  72.1 0.8 gather_fusion.2
  72.9 0.1 copy.58
  73.0 0.2 copy.59
  73.2 0.8 gather_fusion.3
  74.0 0.1 copy.60
  74.1 0.3 pad_maximum_fusion.5
  74.4 0.3 add_dynamic-update-slice_fusion.1
  74.7 0.1 multiply_dynamic-update-slice_fusion.5
  74.8 0.2 multiply_dynamic-update-slice_fusion.2
  75.1 0.2 multiply_dynamic-update-slice_fusion.3
  75.3 0.1 slice.216
  75.4 0.1 multiply_dynamic-update-slice_fusion.1
  75.5 0.1 multiply_dynamic-update-slice_fusion
  75.6 0.7 fusion.49
  76.4 0.0 copy-start.3
  76.4 1.9 %fusion.27 = f32[4,5,129,128]{3,0,2,1:T(4,128)} fusion(f32[4,5,130,128]{3,0,2,1:T(4,128)S(1)} %multiply_dynamic-update-slice_fusion, f32[4,5,1,128]{3,0,2,1:T(4,128)S(1)} %get-tuple-element.49, f32[4,5,128,128]{3,0,2,1:T(4,128)S(1)} %fusion.35, f32[4,5,1,128]{3,0,2,1:T(4,128)S(1)} %get-tuple-element.50, f32[4]{0:T(128)S(1)} %multiply_multiply_fusion), kind=kLoop, calls=%fused_computation.30 | loop fusion | flops 2972160 | bytes 5294096 | tf_op jit(solution)/shard_map/sub | solution.py:74
  78.3 4.3 %fusion.9 = f32[4,5,128,129]{3,0,2,1:T(4,128)} fusion(f32[4,5,128,128]{3,0,2,1:T(4,128)S(1)} %slice.216, f32[4,5,128,1]{3,0,2,1:T(4,128)S(1)} %get-tuple-element.28, f32[4,5,128,1]{3,0,2,1:T(4,128)S(1)} %get-tuple-element.27, f32[4,5,128,1]{3,0,2,1:T(4,128)S(1)} %copy-done.4, f32[4,5,128,128]{3,0,2,1:T(4,128)S(1)} %fusion.35, f32[4,5,128,1]{3,0,2,1:T(4,128)S(1)} %copy-done.3), kind=kLoop, calls=%fused_computation.17 | loop fusion | flops 3632640 | bytes 3983360 | tf_op jit(solution)/shard_map/sub | solution.py:74
  82.6 23.8 %all-gather.5.cloned.1.call-done = f32[16,5,128,128]{3,2,1,0:T(8,128)} async-done(((f32[4,5,128,128]{3,2,1,0:T(8,128)}), f32[16,5,128,128]{3,2,1,0:T(8,128)}) %all-gather.5.cloned.1.call-update) | async-done | bytes 5242896 | tf_op jit(solution)/shard_map/all_gather | solution.py:120
  106.4 11.9 %multiply_add_fusion = (f32[4,5,128,128]{3,0,2,1:T(4,128)S(1)}, f32[4,5,128,128]{3,0,2,1:T(4,128)S(1)}) fusion(f32[4,5,128,128]{3,2,1,0:T(8,128)S(1)} %copy-done, f32[16,5,128,128]{3,2,1,0:T(8,128)} %all-gather.5.cloned.1.call-done, f32[16,16]{1,0:T(8,128)S(1)} %fusion.39, s32[]{:T(128)S(6)} %select_n.46, s32[16,16]{1,0:T(8,128)S(1)} %add_select_fusion, ...), kind=kOutput, calls=%fused_computation.48 | convolution fusion | flops 65536576 | bytes 14424068 | tf_op jit(solution)/shard_map/nm,mvjk->nvjk/dot_general | solution.py:117
  118.3 1.2 copy.64
  119.5 1.2 copy.65
  (27 shorter events, 0.2 us)
Async XLA Ops:
  7.2 7.0 %copy-start = (f32[4,5,128,128]{3,2,1,0:T(8,128)S(1)}, f32[4,5,128,128]{3,2,1,0:T(8,128)}, u32[]{:S(2)}) copy-start(f32[4,5,128,128]{3,2,1,0:T(8,128)} %param.8) | copy-start | bytes 3932164
  7.2 45.6 %all-gather.3.cloned.1.call-start = ((), (), s32[]{:S(2)}) async-start(), calls=%async_computation | async-start | bytes 6553600 | tf_op jit(solution)/shard_map/all_gather | solution.py:120
  7.9 7.7 %copy-start.5 = (s32[1,2,128]{2,1,0:T(2,128)S(1)}, s32[1,2,128]{2,1,0:T(2,128)}, u32[]{:S(2)}) copy-start(s32[1,2,128]{2,1,0:T(2,128)} %param.11) | copy-start | bytes 3076
  7.9 98.5 %all-gather.5.cloned.1.call-start = ((), (), s32[]{:S(2)}) async-start(), calls=%async_computation.1 | async-start | bytes 6553600 | tf_op jit(solution)/shard_map/all_gather | solution.py:120
  8.9 6.8 %copy-start.6 = (s32[4]{0:T(128)S(1)}, s32[4]{0:T(128)}, u32[]{:S(2)}) copy-start(s32[4]{0:T(128)} %param.10) | copy-start | bytes 52
  8.9 7.4 %copy-start.7 = (f32[4]{0:T(128)S(1)}, f32[4]{0:T(128)}, u32[]{:S(2)}) copy-start(f32[4]{0:T(128)} %param.12) | copy-start | bytes 52
  8.9 8.7 %copy-start.8 = (f32[4]{0:T(128)S(1)}, f32[4]{0:T(128)}, u32[]{:S(2)}) copy-start(f32[4]{0:T(128)} %param.13) | copy-start | bytes 52
  8.9 13.6 %collective-permute-start = (f32[4,5,1,128]{3,2,1,0:T(1,128)S(1)}, f32[4,5,1,128]{3,2,1,0:T(1,128)S(1)}, u32[]{:S(2)}, u32[]{:S(2)}) collective-permute-start(f32[4,5,1,128]{3,2,1,0:T(1,128)S(1)} %get-tuple-element.43), channel_id=1, source_target_pairs={{0,4},{4,8},{8,12},{12,0},{1,5},{5,9},{9,13},{13,1},{2,6},{6,10},{... | collective-permute-start | bytes 30728 | tf_op jit(solution)/shard_map/ppermute | solution.py:21
  12.0 11.5 %collective-permute-start.1 = (f32[4,5,1,128]{3,2,1,0:T(1,128)S(1)}, f32[4,5,1,128]{3,2,1,0:T(1,128)S(1)}, u32[]{:S(2)}, u32[]{:S(2)}) collective-permute-start(f32[4,5,1,128]{3,2,1,0:T(1,128)S(1)} %get-tuple-element.44), channel_id=1, source_target_pairs={{4,0},{8,4},{12,8},{0,12},{5,1},{9,5},{13,9},{1,13},{6,2},{10,6},{... | collective-permute-start | bytes 30728 | tf_op jit(solution)/shard_map/ppermute | solution.py:22
  26.9 1.9 %copy-start.1 = (f32[4,5,128,1]{3,0,2,1:T(4,128)S(1)}, f32[4,5,128,1]{3,0,2,1:T(4,128)}, u32[]{:S(2)}) copy-start(f32[4,5,128,1]{3,0,2,1:T(4,128)} %get-tuple-element.41) | copy-start | bytes 30724
  27.0 2.0 %copy-start.2 = (f32[4,5,128,1]{3,0,2,1:T(4,128)S(1)}, f32[4,5,128,1]{3,0,2,1:T(4,128)}, u32[]{:S(2)}) copy-start(f32[4,5,128,1]{3,0,2,1:T(4,128)} %get-tuple-element.42) | copy-start | bytes 30724
  65.8 6.1 %collective-permute-start.2 = (f32[4,5,1,128]{3,0,2,1:T(4,128)S(1)}, f32[4,5,1,128]{3,0,2,1:T(4,128)S(1)}, u32[]{:S(2)}, u32[]{:S(2)}) collective-permute-start(f32[4,5,1,128]{3,0,2,1:T(4,128)S(1)} %get-tuple-element.39), channel_id=1, source_target_pairs={{0,4},{4,8},{8,12},{12,0},{1,5},{5,9},{9,13},{13,1},{2,6},{6,10},{... | collective-permute-start | bytes 30728 | tf_op jit(solution)/shard_map/ppermute | solution.py:21
  67.3 5.6 %collective-permute-start.3 = (f32[4,5,1,128]{3,0,2,1:T(4,128)S(1)}, f32[4,5,1,128]{3,0,2,1:T(4,128)S(1)}, u32[]{:S(2)}, u32[]{:S(2)}) collective-permute-start(f32[4,5,1,128]{3,0,2,1:T(4,128)S(1)} %get-tuple-element.40), channel_id=1, source_target_pairs={{4,0},{8,4},{12,8},{0,12},{5,1},{9,5},{13,9},{1,13},{6,2},{10,6},{... | collective-permute-start | bytes 30728 | tf_op jit(solution)/shard_map/ppermute | solution.py:22
  76.4 1.9 %copy-start.3 = (f32[4,5,128,1]{3,0,2,1:T(4,128)S(1)}, f32[4,5,128,1]{3,0,2,1:T(4,128)}, u32[]{:S(2)}) copy-start(f32[4,5,128,1]{3,0,2,1:T(4,128)} %get-tuple-element.37) | copy-start | bytes 30724
  76.4 1.9 %copy-start.4 = (f32[4,5,128,1]{3,0,2,1:T(4,128)S(1)}, f32[4,5,128,1]{3,0,2,1:T(4,128)}, u32[]{:S(2)}) copy-start(f32[4,5,128,1]{3,0,2,1:T(4,128)} %get-tuple-element.38) | copy-start | bytes 30724
Sparse Core Ops, SparseCore 0:
  9.6 43.1 all-gather.2
  65.9 40.4 all-gather.4
where the time goes:
time: 128 us
  waiting for transfers between devices  43.9 us (34%)
  matrix products  23.7 us (19%)
  other arithmetic  19.8 us (15%)
  local copies, waits for them, and re-layouts  15.9 us (12%)
  between operations  15.1 us (12%)
  starting transfers between devices  9.12 us (7%)
    all_gather x2, waiting for transfers between devices, spectral_of(): lax.all_gather(field, 'inst', axis=0, tiled=True)  43.2 us
    dot_general x2, matrix products, spectral_of(): jnp.einsum('nm,mvjk->nvjk', own_rows, lax.all_gather(field, 'inst', axis=...  23.7 us
    sub x4, other arithmetic, face_terms(): 0.5 * (flux_left + flux_right) - speed * 0.5 * (left + right)  12.4 us
    ppermute x2, starting transfers between devices, padded_2(): before = lax.ppermute(last, axis, up)  4.62 us
    slice x2, local copies, waits for them, and re-layouts, local_residual(): field[..., :1]  4.51 us
    ppermute x2, starting transfers between devices, padded_2(): after = lax.ppermute(initial, axis, down)  4.43 us
    unnamed x23, local copies, waits for them, and re-layouts  3.41 us
  transfers between devices with their start and end apart: 6, of which 2 were waited for; matrix products, arithmetic and copies ran while one was open for 25% of the time, Pallas kernels for 0%

commit v1 on v0

--- a/solution.py
+++ b/solution.py
@@ -9,6 +9,22 @@
 TIME_STEP = 0.05
 DISSIPATION = 2.0
 FREQUENCY = 0.5
+
+
+def gather_around(x, axis, dim):
+    ways, here, step = (lax.axis_size(axis), lax.axis_index(axis), x.shape[dim])
+    shape = [n * ways if d == dim else n for d, n in enumerate(x.shape)]
+    full = lax.dynamic_update_slice_in_dim(jnp.zeros(shape, x.dtype), x, here * step, axis=dim)
+    going_up = going_down = x
+    for far in range(1, ways // 2 + 1):
+        going_up = lax.ppermute(going_up, axis, [(d, (d + 1) % ways) for d in range(ways)])
+        full = lax.dynamic_update_slice_in_dim(full, going_up, (here - far) % ways * step, axis=dim)
+        if 2 * far < ways:
+            going_down = lax.ppermute(going_down, axis, [(d, (d - 1) % ways) for d in range(ways)])
+            full = lax.dynamic_update_slice_in_dim(
+                full, going_down, (here + far) % ways * step, axis=dim
+            )
+    return full
 
 
 def padded_2(shard, sides, width):
@@ -117,7 +133,7 @@
         return jnp.einsum(
             "nm,mvjk->nvjk",
             own_rows,
-            lax.all_gather(field, "inst", axis=0, tiled=True),
+            gather_around(field, "inst", 0),
             precision=lax.Precision.HIGHEST,
         )
 

time: 128 us -> 116 us (0.906)
  local copies, waits for them, and re-layouts: 15.9 us -> 33.8 us
  between operations: 15.1 us -> 1.74 us
  matrix products: 23.7 us -> 12 us
  waiting for transfers between devices: 43.9 us -> 34.4 us
  starting transfers between devices: 9.12 us -> 16 us
  other arithmetic: 19.8 us -> 18.1 us
    all_gather x2 -> x0, waiting for transfers between devices: 43.2 us -> none  [spectral_of(): lax.all_gather(field, 'inst', axis=0, tiled=True)]
    ppermute x0 -> x6, waiting for transfers between devices: none -> 34.4 us  [the longest x4 34.4 us: gather_around(): lax.ppermute(going_up, axis, [(d, (d + 1) % ways) for d in range(ways)])]
    dynamic_update_slice x0 -> x6, local copies, waits for them, and re-layouts: none -> 12.2 us  [the longest x4 7.24 us: gather_around(): lax.dynamic_update_slice_in_dim(full, going_up, (here - far) % ways * ste...]
    dot_general x2, matrix products: 23.7 us -> 12 us  [spectral_of(): jnp.einsum('nm,mvjk->nvjk', own_rows, gather_around(field, 'inst', 0), pr...]
    ppermute x0 -> x6, starting transfers between devices: none -> 7.69 us  [the longest x4 5.64 us: gather_around(): lax.ppermute(going_up, axis, [(d, (d + 1) % ways) for d in range(ways)])]
    sub x4, other arithmetic: 12.4 us -> 8.2 us  [face_terms(): 0.5 * (flux_left + flux_right) - speed * 0.5 * (left + right)]
    unnamed x23 -> x21, local copies, waits for them, and re-layouts: 3.41 us -> 7.05 us
    another operation x0 -> x2, local copies, waits for them, and re-layouts: none -> 3.22 us
  transfers between devices with their start and end apart: 6 -> 10, of which waited for: 2 -> 4; matrix products, arithmetic and copies ran while one was open for 25% -> 38% of each run, Pallas kernels for 0% -> 0%
where the time goes in v1:
time: 116 us
  waiting for transfers between devices  34.4 us (30%)
  local copies, waits for them, and re-layouts  33.8 us (29%)
  other arithmetic  18.1 us (16%)
  starting transfers between devices  16 us (14%)
  matrix products  12 us (10%)
  between operations  1.74 us (2%)
    ppermute x4, waiting for transfers between devices, gather_around(): lax.ppermute(going_up, axis, [(d, (d + 1) % ways) for d in range(ways)])  34.4 us
    dot_general x2, matrix products, spectral_of(): jnp.einsum('nm,mvjk->nvjk', own_rows, gather_around(field, 'inst', 0), pr...  12 us
    sub x4, other arithmetic, face_terms(): 0.5 * (flux_left + flux_right) - speed * 0.5 * (left + right)  8.2 us
    dynamic_update_slice x4, local copies, waits for them, and re-layouts, gather_around(): lax.dynamic_update_slice_in_dim(full, going_up, (here - far) % ways * ste...  7.24 us
    unnamed x21, local copies, waits for them, and re-layouts  7.05 us
    ppermute x4, starting transfers between devices, gather_around(): lax.ppermute(going_up, axis, [(d, (d + 1) % ways) for d in range(ways)])  5.64 us
    dynamic_update_slice x2, local copies, waits for them, and re-layouts, gather_around(): lax.dynamic_update_slice_in_dim(full, going_down, (here + far) % ways * s...  4.96 us
    ppermute x2, starting transfers between devices, padded_2(): after = lax.ppermute(initial, axis, down)  4.86 us
  transfers between devices with their start and end apart: 10, of which 4 were waited for; matrix products, arithmetic and copies ran while one was open for 38% of the time, Pallas kernels for 0%

profile of v1, /device:TPU:0, one launch (start us, length us, event | category | flops | bytes accessed | tf_op | source)
XLA Modules:
  0.0 116.0 jit_solution(16949332957205578946)
XLA Ops:
  0.6 0.5 collective-permute-start.2
  1.1 2.0 %collective-permute-start.3 = (f32[4,5,128,128]{3,2,1,0:T(8,128)}, f32[4,5,128,128]{3,2,1,0:T(8,128)}, u32[]{:S(2)}, u32[]{:S(2)}) collective-permute-start(f32[4,5,128,128]{3,2,1,0:T(8,128)} %param.8), channel_id=1, source_target_pairs={{0,3},{1,0},{2,1},{3,2},{4,7},{5,4},{6,5},{7,6},{8,11},{9,8},{10,9... | collective-permute-start | bytes 3932168 | tf_op jit(solution)/shard_map/ppermute | solution.py:23
  3.1 1.0 fusion.39
  4.1 2.4 %collective-permute-start = (f32[4,5,1,128]{3,2,1,0:T(1,128)S(1)}, f32[4,5,1,128]{3,2,1,0:T(1,128)S(1)}, u32[]{:S(2)}, u32[]{:S(2)}) collective-permute-start(f32[4,5,1,128]{3,2,1,0:T(1,128)S(1)} %get-tuple-element.41), channel_id=1, source_target_pairs={{0,4},{4,8},{8,12},{12,0},{1,5},{5,9},{9,13},{13,1},{2,6},{6,10},{... | collective-permute-start | bytes 30728 | tf_op jit(solution)/shard_map/ppermute | solution.py:37
  6.5 2.1 %collective-permute-start.1 = (f32[4,5,1,128]{3,2,1,0:T(1,128)S(1)}, f32[4,5,1,128]{3,2,1,0:T(1,128)S(1)}, u32[]{:S(2)}, u32[]{:S(2)}) collective-permute-start(f32[4,5,1,128]{3,2,1,0:T(1,128)S(1)} %get-tuple-element.42), channel_id=1, source_target_pairs={{4,0},{8,4},{12,8},{0,12},{5,1},{9,5},{13,9},{1,13},{6,2},{10,6},{... | collective-permute-start | bytes 30728 | tf_op jit(solution)/shard_map/ppermute | solution.py:38
  9.2 1.3 %fusion.31 = s32[]{:T(128)} fusion(s32[4]{0:T(128)} %param.10, s32[]{:T(128)} %bitcast.42), kind=kLoop, calls=%fused_computation.115 | loop fusion | flops 11 | bytes 24 | tf_op jit(solution)/shard_map/reduce_sum | solution.py:122
  10.5 2.0 %fusion.30 = f32[]{:T(128)} fusion(f32[4]{0:T(128)} %param.13, s32[]{:T(128)} %fusion.31), kind=kLoop, calls=%fused_computation.114 | loop fusion | flops 11 | bytes 24 | tf_op jit(solution)/shard_map/reduce_sum | solution.py:125
  12.5 1.9 %fusion.29 = f32[]{:T(128)} fusion(f32[4]{0:T(128)} %param.12, s32[]{:T(128)} %fusion.31), kind=kLoop, calls=%fused_computation.113 | loop fusion | flops 11 | bytes 24 | tf_op jit(solution)/shard_map/reduce_sum | solution.py:124
  14.4 0.8 compare_and_fusion
  15.2 2.8 %broadcast.105.clone = f32[16,5,128,128]{3,0,2,1:T(8,128)} broadcast(f32[]{:T(128)} %constant.75.clone.1), dimensions={} | broadcast | bytes 5242884 | tf_op jit(solution)/shard_map/broadcast.21
  18.0 2.1 %fusion.40 = (f32[4,5,128,128]{3,0,2,1:T(4,128)S(1)}, f32[16,5,128,128]{3,0,2,1:T(8,128)}) fusion(f32[4,5,128,128]{3,2,1,0:T(8,128)S(1)} %copy-done.1, f32[16,5,128,128]{3,0,2,1:T(8,128)} %broadcast.105.clone, s32[]{:T(128)S(6)} %select_n.80), kind=kLoop, calls=%fused_computation.123 | loop fusion | bytes 3932164 | tf_op args[0]
  20.1 2.2 %fusion.38 = (f32[4,5,128,1]{3,0,2,1:T(4,128)}, f32[4,5,128,1]{3,0,2,1:T(4,128)}) fusion(f32[4,5,128,128]{3,0,2,1:T(4,128)S(1)} %get-tuple-element.43), kind=kLoop, calls=%fused_computation.121 | loop fusion | bytes 40960 | tf_op jit(solution)/shard_map/slice | solution.py:100
  22.3 1.2 %multiply_multiply_fusion = f32[4]{0:T(128)S(1)} fusion(f32[]{:T(128)} %fusion.30, s32[]{:T(128)S(6)} %mul.304, f32[]{:T(128)} %fusion.29), kind=kLoop, calls=%fused_computation.116 | loop fusion | flops 24 | bytes 28 | tf_op jit(solution)/shard_map/mul | solution.py:91
  23.6 0.2 copy.50
  23.8 0.8 gather_fusion.1
  24.6 0.1 copy.28
  24.7 0.2 copy.49
  24.9 0.8 gather_fusion
  25.8 0.3 pad_maximum_fusion.4
  26.1 0.3 add_dynamic-update-slice_fusion.3
  26.4 0.1 multiply_dynamic-update-slice_fusion.11
  26.5 0.2 multiply_dynamic-update-slice_fusion.8
  26.8 0.2 multiply_dynamic-update-slice_fusion.9
  27.1 0.1 multiply_dynamic-update-slice_fusion.6
  27.2 0.7 fusion.15
  27.9 2.1 %collective-permute-done.2 = f32[4,5,128,128]{3,2,1,0:T(8,128)} collective-permute-done((f32[4,5,128,128]{3,2,1,0:T(8,128)}, f32[4,5,128,128]{3,2,1,0:T(8,128)}, u32[]{:S(2)}, u32[]{:S(2)}) %collective-permute-start.2) | collective-permute-done | bytes 1310752 | tf_op jit(solution)/shard_map/ppermute | solution.py:20
  30.1 2.5 %collective-permute-start.4 = (f32[4,5,128,128]{3,2,1,0:T(8,128)}, f32[4,5,128,128]{3,2,1,0:T(8,128)S(1)}, u32[]{:S(2)}, u32[]{:S(2)}) collective-permute-start(f32[4,5,128,128]{3,2,1,0:T(8,128)} %collective-permute-done.2), channel_id=1, source_target_pairs={{0,1},{1,2},{2,3},{3,0},{4,5},{5,6},{6,7},{7,4},{8,9},{9,10},{10,1... | collective-permute-start | bytes 3932168 | tf_op jit(solution)/shard_map/ppermute | solution.py:20
  32.6 0.8 fusion.35
  33.4 1.2 %copy-done.2 = f32[4,5,128,1]{3,0,2,1:T(4,128)S(1)} copy-done((f32[4,5,128,1]{3,0,2,1:T(4,128)S(1)}, f32[4,5,128,1]{3,0,2,1:T(4,128)}, u32[]{:S(2)}) %copy-start.2) | copy-done | bytes 10264
  34.6 0.4 copy-done.3
  35.0 3.4 %fusion.2 = f32[4,5,128,129]{3,0,2,1:T(4,128)S(1)} fusion(f32[4,5,128,128]{3,0,2,1:T(4,128)S(1)} %slice.198, f32[4,5,128,1]{3,0,2,1:T(4,128)S(1)} %get-tuple-element.31, f32[4,5,128,1]{3,0,2,1:T(4,128)S(1)} %get-tuple-element.30, f32[4,5,128,1]{3,0,2,1:T(4,128)S(1)} %copy-done.3, f32[4,5,128,128]{3,0,2,1:T(4,128)S(1)} %get-tuple-element.43, ...), kind=kLoop, calls=%fused_computation.7 | loop fusion | flops 3632640 | bytes 3983360 | tf_op jit(solution)/shard_map/sub | solution.py:90
  38.4 3.3 %copy_dynamic-update-slice_fusion.2 = f32[16,5,128,128]{3,0,2,1:T(8,128)} fusion(f32[16,5,128,128]{3,0,2,1:T(8,128)} %get-tuple-element.44, s32[]{:T(128)S(6)} %select_n.82, f32[4,5,128,128]{3,2,1,0:T(8,128)} %collective-permute-done.2), kind=kLoop, calls=%fused_computation.46 | loop fusion | bytes 2621444 | tf_op jit(solution)/shard_map/dynamic_update_slice | solution.py:21
  41.7 3.3 %copy_dynamic-update-slice_fusion.1 = f32[16,5,128,128]{3,0,2,1:T(8,128)} fusion(f32[16,5,128,128]{3,0,2,1:T(8,128)} %copy_dynamic-update-slice_fusion.2, s32[]{:T(128)S(6)} %select_n.84, f32[4,5,128,128]{3,2,1,0:T(8,128)} %collective-permute-done.3), kind=kLoop, calls=%fused_computation.45 | loop fusion | bytes 2621444 | tf_op jit(solution)/shard_map/dynamic_update_slice | solution.py:24
  45.0 2.3 %collective-permute-done.4 = f32[4,5,128,128]{3,2,1,0:T(8,128)S(1)} collective-permute-done((f32[4,5,128,128]{3,2,1,0:T(8,128)}, f32[4,5,128,128]{3,2,1,0:T(8,128)S(1)}, u32[]{:S(2)}, u32[]{:S(2)}) %collective-permute-start.4) | collective-permute-done | bytes 1310752 | tf_op jit(solution)/shard_map/ppermute | solution.py:20
  47.3 2.0 %copy_dynamic-update-slice_fusion = f32[16,5,128,128]{3,0,2,1:T(8,128)} fusion(f32[16,5,128,128]{3,0,2,1:T(8,128)} %copy_dynamic-update-slice_fusion.1, s32[]{:T(128)S(6)} %select_n.86, f32[4,5,128,128]{3,2,1,0:T(8,128)S(1)} %collective-permute-done.4), kind=kLoop, calls=%fused_computation.44 | loop fusion | bytes 2621444 | tf_op jit(solution)/shard_map/dynamic_update_slice | solution.py:21
  49.3 0.4 broadcast.105
  49.8 7.2 %constant_dynamic-update-slice_fusion.3 = (f32[16,5,128,128]{3,0,2,1:T(8,128)S(1)}, f32[4,5,128,128]{3,0,2,1:T(4,128)S(1)}) fusion(f32[16,5,128,128]{3,0,2,1:T(8,128)S(1)} %broadcast.105, s32[]{:T(128)S(6)} %select_n.80, f32[16,5,128,128]{3,0,2,1:T(8,128)} %copy_dynamic-update-slice_fusion, f32[16,16]{1,0:T(8,128)S(1)} %fusion.21, ...), kind=kOutput, calls=%fused_computation.97 | convolution fusion | flops 65536576 | bytes 14425088 | tf_op jit(solution)/shard_map/nm,mvjk->nvjk/dot_general | solution.py:133
  57.0 2.6 %collective-permute-start.7 = (f32[4,5,128,128]{3,0,2,1:T(4,128)S(1)}, f32[4,5,128,128]{3,0,2,1:T(4,128)}, u32[]{:S(2)}, u32[]{:S(2)}) collective-permute-start(f32[4,5,128,128]{3,0,2,1:T(4,128)S(1)} %get-tuple-element.48), channel_id=1, source_target_pairs={{0,1},{1,2},{2,3},{3,0},{4,5},{5,6},{6,7},{7,4},{8,9},{9,10},{10,1... | collective-permute-start | bytes 3932168 | tf_op jit(solution)/shard_map/ppermute | solution.py:20
  59.6 1.1 collective-permute-start.5
  60.7 2.8 %collective-permute-start.6 = (f32[4,5,1,128]{3,0,2,1:T(4,128)S(1)}, f32[4,5,1,128]{3,0,2,1:T(4,128)S(1)}, u32[]{:S(2)}, u32[]{:S(2)}) collective-permute-start(f32[4,5,1,128]{3,0,2,1:T(4,128)S(1)} %get-tuple-element.38), channel_id=1, source_target_pairs={{4,0},{8,4},{12,8},{0,12},{5,1},{9,5},{13,9},{1,13},{6,2},{10,6},{... | collective-permute-start | bytes 30728 | tf_op jit(solution)/shard_map/ppermute | solution.py:38
  63.5 2.2 %fusion.36 = (f32[4,5,128,1]{3,0,2,1:T(4,128)}, f32[4,5,128,1]{3,0,2,1:T(4,128)}) fusion(f32[4,5,128,128]{3,0,2,1:T(4,128)S(1)} %get-tuple-element.48), kind=kLoop, calls=%fused_computation.119 | loop fusion | bytes 40960 | tf_op jit(solution)/shard_map/slice | solution.py:100
  65.7 0.2 copy.43
  65.9 0.8 gather_fusion.3
  66.8 0.2 copy.41
  67.0 0.8 gather_fusion.2
  67.9 0.3 pad_maximum_fusion.5
  68.2 0.3 add_dynamic-update-slice_fusion.1
  68.5 0.1 multiply_dynamic-update-slice_fusion.5
  68.6 0.2 multiply_dynamic-update-slice_fusion.2
  68.8 0.2 multiply_dynamic-update-slice_fusion.3
  69.1 0.7 fusion.34
  69.9 21.3 %collective-permute-done.7 = f32[4,5,128,128]{3,0,2,1:T(4,128)} collective-permute-done((f32[4,5,128,128]{3,0,2,1:T(4,128)S(1)}, f32[4,5,128,128]{3,0,2,1:T(4,128)}, u32[]{:S(2)}, u32[]{:S(2)}) %collective-permute-start.7) | collective-permute-done | bytes 1310752 | tf_op jit(solution)/shard_map/ppermute | solution.py:20
  91.2 0.1 multiply_dynamic-update-slice_fusion
  91.4 0.7 fusion.12
  92.2 0.5 copy-done.4
  92.6 0.4 copy-done.5
  93.0 3.4 %fusion.5 = f32[4,5,128,129]{3,0,2,1:T(4,128)S(1)} fusion(f32[4,5,128,128]{3,0,2,1:T(4,128)S(1)} %slice.216, f32[4,5,128,1]{3,0,2,1:T(4,128)S(1)} %get-tuple-element.26, f32[4,5,128,1]{3,0,2,1:T(4,128)S(1)} %get-tuple-element.25, f32[4,5,128,1]{3,0,2,1:T(4,128)S(1)} %copy-done.5, f32[4,5,128,128]{3,0,2,1:T(4,128)S(1)} %get-tuple-element.48, ...), kind=kLoop, calls=%fused_computation.13 | loop fusion | flops 3632640 | bytes 3983360 | tf_op jit(solution)/shard_map/sub | solution.py:90
  96.4 1.6 %constant_dynamic-update-slice_fusion.2 = f32[16,5,128,128]{3,0,2,1:T(8,128)S(1)} fusion(f32[16,5,128,128]{3,0,2,1:T(8,128)S(1)} %bitcast.44, f32[4,5,128,128]{3,0,2,1:T(4,128)} %collective-permute-done.7, s32[]{:T(128)S(6)} %select_n.82), kind=kLoop, calls=%fused_computation.96 | loop fusion | bytes 2621444 | tf_op jit(solution)/shard_map/dynamic_update_slice | solution.py:21
  98.1 1.6 %constant_dynamic-update-slice_fusion.1 = f32[16,5,128,128]{3,0,2,1:T(8,128)S(1)} fusion(f32[16,5,128,128]{3,0,2,1:T(8,128)S(1)} %constant_dynamic-update-slice_fusion.2, f32[4,5,128,128]{3,0,2,1:T(4,128)} %collective-permute-done.8, s32[]{:T(128)S(6)} %select_n.84), kind=kLoop, calls=%fused_computation.95 | loop fusion | bytes 2621444 | tf_op jit(solution)/shard_map/dynamic_update_slice | solution.py:24
  99.7 8.7 %collective-permute-done.9 = f32[4,5,128,128]{3,0,2,1:T(4,128)S(1)} collective-permute-done((f32[4,5,128,128]{3,0,2,1:T(4,128)}, f32[4,5,128,128]{3,0,2,1:T(4,128)S(1)}, u32[]{:S(2)}, u32[]{:S(2)}) %collective-permute-start.9) | collective-permute-done | bytes 1310752 | tf_op jit(solution)/shard_map/ppermute | solution.py:20
  108.4 0.3 constant_dynamic-update-slice_fusion
  108.7 4.9 %multiply_add_fusion = (f32[4,5,128,128]{3,0,2,1:T(4,128)S(1)}, f32[4,5,128,128]{3,0,2,1:T(4,128)S(1)}) fusion(f32[4,5,128,128]{3,2,1,0:T(8,128)S(1)} %copy-done.1, f32[16,5,128,128]{3,0,2,1:T(8,128)S(1)} %constant_dynamic-update-slice_fusion, f32[16,16]{1,0:T(8,128)S(1)} %fusion.21, s32[]{:T(128)S(6)} %select_n.80, s32[16,16]{1,0:T(8,128)S(1)} %add_select_fusion, ...), kind=kOutput, calls=%fused_computation.47 | convolution fusion | flops 65536576 | bytes 14424068 | tf_op jit(solution)/shard_map/nm,mvjk->nvjk/dot_general | solution.py:133
  113.6 1.2 %copy.46 = f32[4,5,128,128]{3,2,1,0:T(8,128)} copy(f32[4,5,128,128]{3,0,2,1:T(4,128)S(1)} %get-tuple-element.49) | data formatting | bytes 2621440
  114.8 1.2 %copy.47 = f32[4,5,128,128]{3,2,1,0:T(8,128)} copy(f32[4,5,128,128]{3,0,2,1:T(4,128)S(1)} %get-tuple-element.50) | data formatting | bytes 2621440
  (39 shorter events, 0.9 us)
Async XLA Ops:
  0.6 29.4 %collective-permute-start.2 = (f32[4,5,128,128]{3,2,1,0:T(8,128)}, f32[4,5,128,128]{3,2,1,0:T(8,128)}, u32[]{:S(2)}, u32[]{:S(2)}) collective-permute-start(f32[4,5,128,128]{3,2,1,0:T(8,128)} %param.8), channel_id=1, source_target_pairs={{0,1},{1,2},{2,3},{3,0},{4,5},{5,6},{6,7},{7,4},{8,9},{9,10},{10,1... | collective-permute-start | bytes 3932168 | tf_op jit(solution)/shard_map/ppermute | solution.py:20
  1.1 40.6 %collective-permute-start.3 = (f32[4,5,128,128]{3,2,1,0:T(8,128)}, f32[4,5,128,128]{3,2,1,0:T(8,128)}, u32[]{:S(2)}, u32[]{:S(2)}) collective-permute-start(f32[4,5,128,128]{3,2,1,0:T(8,128)} %param.8), channel_id=1, source_target_pairs={{0,3},{1,0},{2,1},{3,2},{4,7},{5,4},{6,5},{7,6},{8,11},{9,8},{10,9... | collective-permute-start | bytes 3932168 | tf_op jit(solution)/shard_map/ppermute | solution.py:23
  4.1 20.6 %collective-permute-start = (f32[4,5,1,128]{3,2,1,0:T(1,128)S(1)}, f32[4,5,1,128]{3,2,1,0:T(1,128)S(1)}, u32[]{:S(2)}, u32[]{:S(2)}) collective-permute-start(f32[4,5,1,128]{3,2,1,0:T(1,128)S(1)} %get-tuple-element.41), channel_id=1, source_target_pairs={{0,4},{4,8},{8,12},{12,0},{1,5},{5,9},{9,13},{13,1},{2,6},{6,10},{... | collective-permute-start | bytes 30728 | tf_op jit(solution)/shard_map/ppermute | solution.py:37
  6.5 17.1 %collective-permute-start.1 = (f32[4,5,1,128]{3,2,1,0:T(1,128)S(1)}, f32[4,5,1,128]{3,2,1,0:T(1,128)S(1)}, u32[]{:S(2)}, u32[]{:S(2)}) collective-permute-start(f32[4,5,1,128]{3,2,1,0:T(1,128)S(1)} %get-tuple-element.42), channel_id=1, source_target_pairs={{4,0},{8,4},{12,8},{0,12},{5,1},{9,5},{13,9},{1,13},{6,2},{10,6},{... | collective-permute-start | bytes 30728 | tf_op jit(solution)/shard_map/ppermute | solution.py:38
  15.2 2.8 %copy-start.1 = (f32[4,5,128,128]{3,2,1,0:T(8,128)S(1)}, f32[4,5,128,128]{3,2,1,0:T(8,128)}, u32[]{:S(2)}) copy-start(f32[4,5,128,128]{3,2,1,0:T(8,128)} %param.8) | copy-start | bytes 3932164
  30.1 17.2 %collective-permute-start.4 = (f32[4,5,128,128]{3,2,1,0:T(8,128)}, f32[4,5,128,128]{3,2,1,0:T(8,128)S(1)}, u32[]{:S(2)}, u32[]{:S(2)}) collective-permute-start(f32[4,5,128,128]{3,2,1,0:T(8,128)} %collective-permute-done.2), channel_id=1, source_target_pairs={{0,1},{1,2},{2,3},{3,0},{4,5},{5,6},{6,7},{7,4},{8,9},{9,10},{10,1... | collective-permute-start | bytes 3932168 | tf_op jit(solution)/shard_map/ppermute | solution.py:20
  33.3 1.3 %copy-start.2 = (f32[4,5,128,1]{3,0,2,1:T(4,128)S(1)}, f32[4,5,128,1]{3,0,2,1:T(4,128)}, u32[]{:S(2)}) copy-start(f32[4,5,128,1]{3,0,2,1:T(4,128)} %get-tuple-element.39) | copy-start | bytes 30724
  33.3 1.7 %copy-start.3 = (f32[4,5,128,1]{3,0,2,1:T(4,128)S(1)}, f32[4,5,128,1]{3,0,2,1:T(4,128)}, u32[]{:S(2)}) copy-start(f32[4,5,128,1]{3,0,2,1:T(4,128)} %get-tuple-element.40) | copy-start | bytes 30724
  56.9 8.8 %copy-start = (f32[16,5,128,128]{3,0,2,1:T(8,128)}, f32[16,5,128,128]{3,0,2,1:T(8,128)S(1)}, u32[]{:S(2)}) copy-start(f32[16,5,128,128]{3,0,2,1:T(8,128)S(1)} %get-tuple-element.47) | copy-start | bytes 15728644
  57.0 41.1 %collective-permute-start.8 = (f32[4,5,128,128]{3,0,2,1:T(4,128)S(1)}, f32[4,5,128,128]{3,0,2,1:T(4,128)}, u32[]{:S(2)}, u32[]{:S(2)}) collective-permute-start(f32[4,5,128,128]{3,0,2,1:T(4,128)S(1)} %get-tuple-element.48), channel_id=1, source_target_pairs={{0,3},{1,0},{2,1},{3,2},{4,7},{5,4},{6,5},{7,6},{8,11},{9,8},{10,9... | collective-permute-start | bytes 3932168 | tf_op jit(solution)/shard_map/ppermute | solution.py:23
  57.0 34.2 %collective-permute-start.7 = (f32[4,5,128,128]{3,0,2,1:T(4,128)S(1)}, f32[4,5,128,128]{3,0,2,1:T(4,128)}, u32[]{:S(2)}, u32[]{:S(2)}) collective-permute-start(f32[4,5,128,128]{3,0,2,1:T(4,128)S(1)} %get-tuple-element.48), channel_id=1, source_target_pairs={{0,1},{1,2},{2,3},{3,0},{4,5},{5,6},{6,7},{7,4},{8,9},{9,10},{10,1... | collective-permute-start | bytes 3932168 | tf_op jit(solution)/shard_map/ppermute | solution.py:20
  59.6 7.1 %collective-permute-start.5 = (f32[4,5,1,128]{3,0,2,1:T(4,128)S(1)}, f32[4,5,1,128]{3,0,2,1:T(4,128)S(1)}, u32[]{:S(2)}, u32[]{:S(2)}) collective-permute-start(f32[4,5,1,128]{3,0,2,1:T(4,128)S(1)} %get-tuple-element.37), channel_id=1, source_target_pairs={{0,4},{4,8},{8,12},{12,0},{1,5},{5,9},{9,13},{13,1},{2,6},{6,10},{... | collective-permute-start | bytes 30728 | tf_op jit(solution)/shard_map/ppermute | solution.py:37
  60.7 5.0 %collective-permute-start.6 = (f32[4,5,1,128]{3,0,2,1:T(4,128)S(1)}, f32[4,5,1,128]{3,0,2,1:T(4,128)S(1)}, u32[]{:S(2)}, u32[]{:S(2)}) collective-permute-start(f32[4,5,1,128]{3,0,2,1:T(4,128)S(1)} %get-tuple-element.38), channel_id=1, source_target_pairs={{4,0},{8,4},{12,8},{0,12},{5,1},{9,5},{13,9},{1,13},{6,2},{10,6},{... | collective-permute-start | bytes 30728 | tf_op jit(solution)/shard_map/ppermute | solution.py:38
  91.2 17.2 %collective-permute-start.9 = (f32[4,5,128,128]{3,0,2,1:T(4,128)}, f32[4,5,128,128]{3,0,2,1:T(4,128)S(1)}, u32[]{:S(2)}, u32[]{:S(2)}) collective-permute-start(f32[4,5,128,128]{3,0,2,1:T(4,128)} %collective-permute-done.7), channel_id=1, source_target_pairs={{0,1},{1,2},{2,3},{3,0},{4,5},{5,6},{6,7},{7,4},{8,9},{9,10},{10,1... | collective-permute-start | bytes 3932168 | tf_op jit(solution)/shard_map/ppermute | solution.py:20
  91.3 1.3 %copy-start.4 = (f32[4,5,128,1]{3,0,2,1:T(4,128)S(1)}, f32[4,5,128,1]{3,0,2,1:T(4,128)}, u32[]{:S(2)}) copy-start(f32[4,5,128,1]{3,0,2,1:T(4,128)} %get-tuple-element.35) | copy-start | bytes 30724
  91.3 1.7 %copy-start.5 = (f32[4,5,128,1]{3,0,2,1:T(4,128)S(1)}, f32[4,5,128,1]{3,0,2,1:T(4,128)}, u32[]{:S(2)}) copy-start(f32[4,5,128,1]{3,0,2,1:T(4,128)} %get-tuple-element.36) | copy-start | bytes 30724
  91.4 5.0 %slice-start = ((s8[5242880]{0:T(1024)(128)(4,1)}), s8[4194304]{0:T(1024)(128)(4,1)S(1)}, s32[]{:S(2)}) async-start(s8[5242880]{0:T(1024)(128)(4,1)} %bitcast.43), calls=%async_computation | async-start | bytes 8388608
  93.0 3.4 %slice-start.1 = ((s8[5242880]{0:T(1024)(128)(4,1)}), s8[1048576]{0:T(1024)(128)(4,1)S(1)}, s32[]{:S(2)}) async-start(s8[5242880]{0:T(1024)(128)(4,1)} %bitcast.43), calls=%async_computation.1 | async-start | bytes 2097152
